TPU v7x, 128 devices: a whole 4x4x4 slice. The times are simulated.
128 devices in a mesh: gx: 8 (over z_lo, x), gy: 16 (over y, z_hi, core).
Axes of the slice: x: 4, y: 4, z: 4 (z_hi: 2, z_lo: 2; z = z_hi * 2 + z_lo), core: 2. Of those that a mesh axis runs over, the one named last changes fastest.
Arguments:
- traces: float32 [4096, 2048], P(('gx', 'gy')), may hold values from -0.09375 to 0.09375
- phase_coef: float32 [2, 4], replicated, may hold values from -0.5 to 0.5
Outputs:
- image: float32 [4096, 2048], P(('gx', 'gy'))
All inputs are finite; a program needn't handle non-finite values.
Results may differ from a plain program's by a relative error of at most 0.0003.
Values sent between devices are 32-bit elements; how exact they have to be, the bound alone decides.
A program may use at most 128 MiB of HBM per device.

v0:
```python
import functools

import jax
import jax.numpy as jnp
import numpy as np
from jax import lax
from jax.experimental import pallas as pl
from jax.experimental.pallas import tpu as pltpu
from jax.sharding import PartitionSpec as P

ORDER = 6
LOGICAL = pl.DeviceIdType.LOGICAL
F32 = jnp.float32
BF16 = jnp.bfloat16
AMP = 64.0

NODES = 0.5 * np.cos(np.pi * (2.0 * np.arange(ORDER) + 1.0) / (2.0 * ORDER))


def lagrange(points):
    points = np.asarray(points)[..., None, None]
    same = np.eye(ORDER, dtype=bool)
    spread = np.where(same, 1.0, NODES[:, None] - NODES[None, :])
    return np.where(same, 1.0, (points - NODES[None, :]) / spread).prod(-1)


CENTRE = lagrange(0.0)
HALVES = np.stack([((side - 0.5) + NODES) * 0.5 for side in (0, 1)])
TABLE = lagrange(HALVES)
WEIGHT = np.transpose(TABLE, (0, 2, 1))


def tail_table():
    out = np.zeros((ORDER, 64, 128))
    for high in range(64):
        total = np.eye(ORDER)
        for place in range(6):
            total = TABLE[(high >> place) & 1] @ total
        out[:, high, :96] = np.repeat(CENTRE[:, None] * total, 16, axis=1)
    return out.astype(np.float32)


def fit(function, terms):
    u = 0.125 + 0.125 * np.cos(np.pi * (np.arange(200) + 0.5) / 200)
    poly = np.polynomial.chebyshev.Chebyshev.fit(u, function(np.sqrt(u)), terms - 1, domain=[0, 0.25])
    return [float(c) for c in poly.convert(kind=np.polynomial.Polynomial).coef]


SIN = fit(lambda r: np.sin(np.pi * r) / r, 5)
SIN2 = [2.0 * c for c in fit(lambda r: np.sin(np.pi * r) / r, 4)]
COS = fit(lambda r: np.cos(np.pi * r), 5)
COS4 = fit(lambda r: np.cos(np.pi * r), 4)


def horner(coefs, u):
    total = coefs[-1]
    for c in coefs[-2::-1]:
        total = total * u + c
    return total


def turn(c):
    r = c - jnp.floor(c + 0.5)
    u = r * r
    twice = r * horner(SIN2, u)
    half_cos = horner(COS4, u)
    return 1.0 - (0.5 * twice) * twice, twice * half_cos


def turn_cos(c):
    r = c - jnp.floor(c + 0.5)
    twice = r * horner(SIN2, r * r)
    return 1.0 - (0.5 * twice) * twice


def half_turn(y):
    r = 0.5 - y
    u = r * r
    return r * horner(SIN, u), horner(COS, u)


def bend_value(coef, row, y):
    cosine = (0.5 - y) * horner(SIN, (0.5 - y) * (0.5 - y))
    c0, c1, c2, c3 = (coef[row, m] for m in range(4))
    return (c0 - c2) + cosine * ((c1 - 3.0 * c3) + cosine * (2.0 * c2 + cosine * (4.0 * c3)))


def bend_terms(coef, size):
    e1, e2, e3 = (coef[0, m] * float(-2.0 * AMP * np.sin(np.pi * m * size / 2.0)) for m in (1, 2, 3))
    return e1 - e3, 2.0 * e2, 4.0 * e3


def bend_step(terms, middle):
    cosine, sine = half_turn(middle)
    return sine * (terms[0] + cosine * (terms[1] + cosine * terms[2]))


def apply_real(weights, values):
    out = []
    for t in range(ORDER):
        total = weights[t][0] * values[0]
        for s in range(1, ORDER):
            total = total + weights[t][s] * values[s]
        out.append(total)
    return out


def iota(axis):
    return lax.broadcasted_iota(jnp.int32, (8, 128), axis)


def asf(value):
    return value.astype(F32)


def div(a, b):
    return lax.div(a, jnp.int32(b))


def rem(a, b):
    return lax.rem(a, jnp.int32(b))


def subset(deltas, mask):
    total = None
    for k, delta in enumerate(deltas):
        if (mask >> k) & 1:
            total = delta if total is None else total + delta
    return 0 if total is None else total


def abs_flip(bit, turned):
    return 1 - bit if turned else bit


def flips(bits, weights):
    return [weight * (1 - 2 * bit) for bit, weight in zip(bits, weights)]


def lane_parts(classes, core):
    lane = iota(1)
    place = lane >> 4
    x, y, z = (
        (2 * c + e + core) & 3 for c, e in zip(classes, (place >> 2, (place >> 1) & 1, place & 1))
    )
    return (z >> 1) + 2 * y + 8 * x + 32 * (z & 1), lane & 15


def early_levels(coef, box, top, w_ref, p_ref, v_ref):
    sub = iota(0)
    bits = [asf(sub & 1), asf((sub >> 1) & 1), asf(sub >> 2)]
    sign = [2.0 * bit - 1.0 for bit in bits]
    x0 = jnp.full((8, 128), 0.5, F32)
    x1 = x0 + sign[0] * 0.25
    x2 = x1 + sign[1] * 0.125
    word4 = asf(box * 16 + top)
    steps = [
        bend_step(bend_terms(coef, 2.0 ** -(level + 1)), x + sign[level - 1] * 2.0 ** -(level + 2))
        for level, x in ((1, x0), (2, x1), (3, x2))
    ]
    p0_mid = coef[0, 0] - coef[0, 2]

    def turned(values, angles):
        pairs = [(a * c - b * d, a * d + b * c) for (a, b), (c, d) in zip(values, angles)]
        return [a for a, _ in pairs], [b for _, b in pairs]

    linear2 = 2.0 * asf(top & 1) + 0.5
    linear3 = asf(top & 3) + 0.5
    third = [turn(sign[2] * ((linear3 + float(NODES[s])) * 0.25 + steps[2] * p_ref[0, s])) for s in range(ORDER)]
    constants = [[float(WEIGHT[0][t][s]) for s in range(ORDER)] for t in range(ORDER)]

    def by_side(side, values):
        mirror = jnp.broadcast_to(side, (8, 128)) == 1
        picked = [jnp.where(mirror, values[5 - s], values[s]) for s in range(ORDER)]
        out = apply_real(constants, picked)
        return [jnp.where(mirror, out[5 - t], out[t]) for t in range(ORDER)]

    def body(group, _):
        j0, j1 = rem(group, 2), div(group, 2)
        j0f, j1f, groupf = asf(j0), asf(j1), asf(group)
        word = word4 * 4.0 + groupf
        start = 0.5 * (j0f + 0.5) + AMP * p0_mid * bend_value(coef, 1, (word + 0.5) * 2.0**-12)
        real, imag = [], []
        for s in range(ORDER):
            node = float(NODES[s])
            p1 = bend_value(coef, 1, (word + (0.5 + node)) * 2.0**-12)
            c, d = turn(start + sign[0] * ((groupf + (0.5 + node)) * 0.25 + steps[0] * p1))
            real.append(c * float(CENTRE[s]))
            imag.append(d * float(CENTRE[s]))
        values = list(zip(by_side(j0, real), by_side(j0, imag)))
        word = word4 * 2.0 + j1f
        angles = []
        for s in range(ORDER):
            node = float(NODES[s])
            p1 = bend_value(coef, 1, (word + (0.5 + node)) * 2.0**-11)
            angles.append(turn(sign[1] * (((linear2 + j1f) + node) * 0.25 + steps[1] * p1)))
        values = list(zip(*(by_side(j1, part) for part in turned(values, angles))))
        weights = [[w_ref[0, ORDER * t + s] for s in range(ORDER)] for t in range(ORDER)]
        for c, part in enumerate(turned(values, third)):
            for t, value in enumerate(apply_real(weights, part)):
                v_ref[0, 2 * t + c, group] = value
        return 0

    lax.fori_loop(0, 4, body, 0)


def late_setup(coef, box, top, w_ref, p_ref, c_ref):
    full = box * 16 + top

    def body(i, scale):
        word = full >> i
        pick = (word & 1) == 1
        for t in range(ORDER):
            for s in range(ORDER):
                w_ref[i, ORDER * t + s] = jnp.where(pick, float(WEIGHT[1][t][s]), float(WEIGHT[0][t][s]))
        for s in range(ORDER):
            p_ref[i, s] = bend_value(coef, 1, (asf(word) + float(0.5 + NODES[s])) * scale)
        return scale * 2.0

    lax.fori_loop(0, 5, body, jnp.float32(2.0**-10))
    turn_of = top & 7

    def by_lane(values):
        out = jnp.full((8, 128), float(values[ORDER - 1]), F32)
        for t in range(ORDER - 1):
            out = jnp.where(turn_of == t, float(values[t]), out)
        return out

    e1, e2, e3 = (coef[0, m] * by_lane(-2.0 * AMP * np.sin(np.pi * m * NODES / 128.0)) for m in (1, 2, 3))
    node = by_lane(NODES)
    c_ref[0] = node
    c_ref[1] = e1 - e3
    c_ref[2] = 2.0 * e2
    c_ref[3] = 4.0 * e3
    c_ref[4] = node * (asf(box) + 0.5)


def spread(value, t):
    return jnp.take_along_axis(value, (iota(1) & 120) + t, axis=1)


def late_levels(coef, box, top, order, w_ref, p_ref, c_ref, v_ref, g_ref, between):
    sub = iota(0)
    x3 = asf(4 * (sub & 1) + (sub & 2) + (sub >> 2)) * 0.125 + 0.0625
    full = box * 16 + top
    terms = [bend_terms(coef, 2.0 ** -(level + 1)) for level in (4, 5, 6)]

    def sign_of(bit):
        return (2 * bit - 1).astype(F32)

    def turns(i, level_terms, shift, parent, sign):
        steps = bend_step(level_terms, parent + sign * shift)
        linear = asf((full >> i) & 3) + 0.5
        return [turn(sign * ((linear + float(NODES[s])) * 0.25 + steps * p_ref[i, s])) for s in range(ORDER)]

    def level_step(level, q3, q4):
        first = level == 4
        i = level - 3
        parent = x3 + jnp.where(first, 0.0, sign_of(q3) * 2.0**-5)
        sign = jnp.where(first, sign_of(q3), sign_of(q4))
        level_terms = [jnp.where(first, a, b) for a, b in zip(terms[0], terms[1])]
        real, imag = [], []
        for s, (c, d) in enumerate(turns(i, level_terms, jnp.where(first, 2.0**-6, 2.0**-7), parent, sign)):
            a, b = v_ref[i - 1, 2 * s], v_ref[i - 1, 2 * s + 1]
            real.append(a * c - b * d)
            imag.append(a * d + b * c)
        weights = [[w_ref[i, ORDER * t + s] for s in range(ORDER)] for t in range(ORDER)]
        for c, values in enumerate((real, imag)):
            for t, value in enumerate(apply_real(weights, values)):
                v_ref[i, 2 * t + c] = value

    def last_step(parent, bit, place):
        sign = sign_of(bit)
        middle = parent + sign * 2.0**-7 + c_ref[0] * (1.0 / 128.0)
        steps = bend_step((c_ref[1], c_ref[2], c_ref[3]), middle)
        switch = [turn((c_ref[4] + c_ref[0] * float(NODES[u])) + steps * p_ref[4, u]) for u in range(ORDER)]
        merged = []
        for s, (c, d) in enumerate(turns(3, terms[2], 2.0**-8, parent, sign)):
            a = b = None
            for u in range(ORDER):
                weight = w_ref[3, ORDER * u + s]
                a = switch[u][0] * weight if a is None else a + switch[u][0] * weight
                b = switch[u][1] * weight if b is None else b + switch[u][1] * weight
            merged.append((a * c - b * d, a * d + b * c))
        parts = [v_ref[2, 2 * s] + v_ref[2, 2 * s + 1] for s in range(ORDER)]
        for t in range(ORDER):
            k1 = k2 = k3 = None
            for s in range(ORDER):
                c, d = spread(merged[s][0], t), spread(merged[s][1], t)
                m1, m2, m3 = parts[s] * c, v_ref[2, 2 * s] * (d - c), v_ref[2, 2 * s + 1] * (c + d)
                k1 = m1 if k1 is None else k1 + m1
                k2 = m2 if k2 is None else k2 + m2
                k3 = m3 if k3 is None else k3 + m3
            real, imag = k1 - k3, k1 + k2
            rows = pl.ds(pl.multiple_of(place * 192 + 16 * t, 16), 16)
            rows_low = pl.ds(pl.multiple_of(place * 192 + 96 + 16 * t, 16), 16)
            for j in range(4):
                both = jnp.concatenate([real[j], imag[j]], axis=0)
                high = both.astype(BF16)
                g_ref[rows, 128 * j : 128 * (j + 1)] = high
                g_ref[rows_low, 128 * j : 128 * (j + 1)] = (both - high.astype(F32)).astype(BF16)

    def over(n, _):
        @pl.when(n >= 4)
        def _():
            between(n - 4)

        @pl.when(n < 4)
        def _():
            q3, q4 = order(div(n, 2)), rem(n, 2)

            def levels(level, _):
                level_step(level, q3, q4)
                return 0

            lax.fori_loop(4 + q4, 6, levels, 0)
            x5 = x3 + (sign_of(q3) * 2.0**-5 + sign_of(q4) * 2.0**-6)

            def over5(q5, _):
                last_step(x5, q5, 4 * q3 + q4 + 2 * q5)
                return 0

            lax.fori_loop(0, 2, over5, 0)

        return 0

    lax.fori_loop(0, 6, over, 0)


def last_weights(coef, group, tail_ref, h_ref):
    sub, lane = iota(0), iota(1)
    own = lane & 7
    same = sub == own
    box6 = 32 * (own & 1) + 8 * (own & 2) + 2 * (own & 4)
    box6 = box6 + (4 * rem(group, 2) + 2 * rem(div(group, 2), 2) + div(group, 4))
    inner = 32 * (sub & 1) + 8 * (sub & 2) + 2 * (sub & 4)
    base = box6 * 64 + inner
    quarter = 0.25 * asf((lane >> 3) & 1)
    p1_mid = coef[1, 0] - coef[1, 2]

    def rows_of(r):
        centre = (asf(base + (4 * rem(r, 2) + 2 * rem(div(r, 2), 2) + div(r, 4))) + 0.5) * 2.0**-12
        total = None
        for t in range(ORDER):
            node = float(NODES[t])
            steps = bend_step(bend_terms(coef, node / 4096.0), centre + node / 8192.0)
            term = turn_cos((quarter - 0.5 * node) - steps * p1_mid)
            term = term * tail_ref[t, pl.ds(pl.multiple_of(8 * r, 8), 8), :]
            total = term if total is None else total + term
        return total

    def body(r, _):
        total = rows_of(r)
        for k in range(0, 8, 2):
            both = jnp.concatenate(
                [jnp.where(same, jnp.broadcast_to(total[k + n : k + n + 1], (8, 128)), 0.0) for n in range(2)], axis=0
            )
            high = both.astype(BF16)
            rows = pl.ds(pl.multiple_of(64 * r + 8 * k, 16), 16)
            h_ref[rows, 0:128] = high
            h_ref[rows, 128:256] = (both - high.astype(F32)).astype(BF16)
            h_ref[rows, 256:384] = high
        return 0

    lax.fori_loop(0, 8, body, 0)


def kernel(
    x_ref,
    coef_hbm,
    tail_hbm,
    out_ref,
    coef_ref,
    tail_ref,
    w_ref,
    p_ref,
    c_ref,
    v_ref,
    g_ref,
    h_ref,
    xr_ref,
    xs_ref,
    part_ref,
    rr_ref,
    sum_ref,
    tile_ref,
    send_sems,
    recv_sems,
):
    fetch_coef = pltpu.make_async_copy(coef_hbm, coef_ref, recv_sems.at[3])
    fetch_tail = pltpu.make_async_copy(tail_hbm, tail_ref, recv_sems.at[4])
    fetch_coef.start()
    fetch_tail.start()
    gx, gy = lax.axis_index("gx"), lax.axis_index("gy")
    core = rem(gy, 2)
    zl, xs = div(gx, 4), rem(gx, 4)
    xh, xl = div(xs, 2), rem(xs, 2)
    yh, yl, zh = div(gy, 8), rem(div(gy, 4), 2), rem(div(gy, 2), 2)
    me = gx * 16 + gy
    highs, lows = (xh, yh, zh), (xl, yl, zl)
    unlike = [h + l - 2 * h * l for h, l in zip(highs, lows)]
    to_a = [16 * (1 - 2 * xl), 4 * (1 - 2 * yl), 64 * (1 - 2 * zl)]
    to_b = [16 * (3 - 2 * xs), 4 * (3 - 2 * (2 * yh + yl)), 2 * (1 - 2 * zh) + 64 * (1 - 2 * zl)]
    to_class = [a + core * (b - a) for a, b in zip(to_a, to_b)]
    to_group = [b + core * (a - b) for a, b in zip(to_a, to_b)]
    to_core = 1 - 2 * core
    class_a, class_b = highs, [1 - d for d in unlike]
    place_a, place_b = lows, [1 - l for l in lows]
    group_a, group_b = [1 - d for d in unlike], [1 - h for h in highs]

    def mine(for_a, for_b):
        return [a + core * (b - a) for a, b in zip(for_a, for_b)]

    def others(for_a, for_b):
        return [b + core * (a - b) for a, b in zip(for_a, for_b)]

    def number(values):
        return values[0] + 2 * values[1] + 4 * values[2]

    classes, groups = mine(class_a, class_b), mine(group_a, group_b)
    target = number(classes)
    block = number(groups) + 8 * core

    barrier = pltpu.get_barrier_semaphore()
    for mask in range(1, 16):
        source = me + subset(to_class + [to_core], mask)
        pl.semaphore_signal(barrier, inc=1, device_id=source, device_id_type=LOGICAL)
    for mask in range(1, 8):
        pl.semaphore_signal(barrier, inc=1, device_id=me + subset(to_group, mask), device_id_type=LOGICAL)
    box, top = lane_parts(classes, core)
    fetch_coef.wait()
    late_setup(coef_ref, box, top, w_ref, p_ref, c_ref)
    pl.semaphore_wait(barrier, 22)

    def columns(m):
        return x_ref.at[:, pl.ds(pl.multiple_of(m * 128, 128), 128)]

    own_slot = 2 * number(mine(place_a, place_b)[::-1]) + core
    other_slot = 2 * number(others(place_a, place_b)[::-1]) + core
    other_groups = others(group_a, group_b)
    other_block = number(other_groups) + 8 * (1 - core)
    for mask in range(7, -1, -1):
        routes = [(other_block, other_groups, other_slot, me + to_core + subset(to_group, mask))]
        if mask:
            routes.append((block, groups, own_slot, me + subset(to_class, mask)))
        for first, group_bits, slot, device in routes:
            pltpu.make_async_remote_copy(
                src_ref=columns(first + subset(flips(group_bits, (1, 2, 4)), mask)),
                dst_ref=xr_ref.at[slot],
                send_sem=send_sems.at[0],
                recv_sem=recv_sems.at[0],
                device_id=device,
                device_id_type=LOGICAL,
            ).start()
    pltpu.make_async_copy(columns(block), xr_ref.at[own_slot], recv_sems.at[0]).start()
    early_levels(coef_ref, box, top, w_ref, p_ref, v_ref)

    def order(h):
        return classes[0] + (1 - h) * (1 - 2 * classes[0])

    def split(i, _):
        for j in range(4):
            piece = jnp.concatenate([xr_ref[2 * i + s, pl.ds(j, 8, stride=4), :] for s in range(2)], axis=0)
            high = piece.astype(BF16)
            rows = pl.ds(pl.multiple_of(128 * j + 16 * i, 16), 16)
            xs_ref[rows, 0:128] = high
            xs_ref[rows, 128:256] = (piece - high.astype(F32)).astype(BF16)
        return 0

    def half(h):
        @pl.when(h == 0)
        def _():
            pltpu.make_async_copy(xr_ref, xr_ref, recv_sems.at[0]).wait()
            lax.fori_loop(0, 8, split, 0, unroll=4)

        q3 = order(h)
        far = (1 - h) * to_group[0]
        for mask in range(3, -1, -1):
            i = classes[1] + 2 * classes[2] + subset(flips(classes[1:], (1, 2)), mask)
            rows = pl.ds(pl.multiple_of((4 * q3 + i) * 192, 16), 192)
            wide = jnp.dot(g_ref[rows, :], xs_ref[...], preferred_element_type=F32)
            part = wide[0:96, 0:128] + (wide[0:96, 128:256] + wide[96:192, 0:128])

            def send():
                part_ref[4 * q3 + i] = part
                pltpu.make_async_remote_copy(
                    src_ref=part_ref.at[4 * q3 + i],
                    dst_ref=rr_ref.at[target],
                    send_sem=send_sems.at[1],
                    recv_sem=recv_sems.at[1],
                    device_id=me + far + subset(to_group[1:], mask),
                    device_id_type=LOGICAL,
                ).start()

            if mask:
                send()
            else:
                pl.when(h == 0)(send)

                @pl.when(h == 1)
                def _():
                    rr_ref[target] = part

    late_levels(coef_ref, box, top, order, w_ref, p_ref, c_ref, v_ref, g_ref, half)
    fetch_tail.wait()
    for i in range(3):
        sum_ref[128 * i + 96 : 128 * i + 128, :] = jnp.zeros((32, 128), BF16)
    last_weights(coef_ref, target, tail_ref, h_ref)
    pltpu.make_async_copy(rr_ref.at[0:7], rr_ref.at[0:7], recv_sems.at[1]).wait()

    def add(i, _):
        rows = pl.ds(pl.multiple_of(16 * i, 16), 16)
        total = rr_ref[0, rows, :]
        for k in range(1, 8):
            total = total + rr_ref[k, rows, :]
        high = total.astype(BF16)
        sum_ref[rows, :] = high
        sum_ref[pl.ds(pl.multiple_of(128 + 16 * i, 16), 16), :] = high
        sum_ref[pl.ds(pl.multiple_of(256 + 16 * i, 16), 16), :] = (total - high.astype(F32)).astype(BF16)
        return 0

    lax.fori_loop(0, 6, add, 0, unroll=True)

    home = zh + 2 * yl + 4 * yh + 8 * xl + 16 * xh + 32 * zl
    own = core == classes[2]
    row = pl.multiple_of((classes[0] + 2 * classes[1]) * 8, 8)
    here = out_ref.at[pl.ds(row, 8), pl.ds(pl.multiple_of(block * 128, 128), 128)]
    turns = flips((zh, xl, xh, yh, yl, zl), (1, 8, 16, 4, 2, 32))

    def deliver(high):
        pltpu.make_async_remote_copy(
            src_ref=tile_ref.at[high],
            dst_ref=here,
            send_sem=send_sems.at[2],
            recv_sem=recv_sems.at[2],
            device_id=2 * high + classes[2],
            device_id_type=LOGICAL,
        ).start()

    early = (0, 8)
    lost = (63 - home, home + subset(turns, 48))
    instead = [jnp.where(lost[n] == early[1 - n], lost[1 - n], lost[n]) for n in range(2)]

    def settle(high):
        return jnp.where(high == early[0], instead[0], jnp.where(high == early[1], instead[1], high))

    tile_ref[...] = jnp.dot(h_ref[...], sum_ref[...], preferred_element_type=F32).reshape(64, 8, 128)
    for high in early:
        pl.when(jnp.logical_or(home != high, jnp.logical_not(own)))(functools.partial(deliver, high))
    moved = jnp.logical_or(home == early[0], home == early[1])
    last = jnp.logical_or(moved, jnp.logical_not(own))

    def deliver_some(step, _):
        same_y, same_z = rem(step, 2), div(step, 2)
        first = home + (1 - same_y) * turns[4] + (1 - same_z) * turns[5]

        def send(mask):
            deliver(settle(first + subset(turns, mask)))

        pl.when(step > 0)(lambda: send(15))
        pl.when(jnp.logical_and(step > 0, jnp.logical_or(step < 3, last)))(lambda: send(0))
        for mask in (14, 1, 13, 2, 12, 3, 11, 4, 10, 5, 9, 6, 8, 7):
            send(mask)
        return 0

    lax.fori_loop(0, 4, deliver_some, 0)

    @pl.when(own)
    def _():
        pltpu.make_async_copy(tile_ref.at[home], here, recv_sems.at[2]).start()

    pltpu.make_async_copy(xr_ref.at[0:15], xr_ref.at[0:15], send_sems.at[0]).wait()
    pltpu.make_async_copy(part_ref.at[0:7], part_ref.at[0:7], send_sems.at[1]).wait()

    @pl.when(own)
    def _():
        pltpu.make_async_copy(tile_ref.at[0:63], tile_ref.at[0:63], send_sems.at[2]).wait()

    @pl.when(jnp.logical_not(own))
    def _():
        pltpu.make_async_copy(tile_ref, tile_ref, send_sems.at[2]).wait()

    pltpu.make_async_copy(out_ref, out_ref, recv_sems.at[2]).wait()


def shards(traces, phase_coef):
    return pl.pallas_call(
        kernel,
        out_shape=jax.ShapeDtypeStruct((32, 2048), F32),
        in_specs=[
            pl.BlockSpec(memory_space=pl.ANY),
            pl.BlockSpec(memory_space=pl.ANY),
            pl.BlockSpec(memory_space=pl.ANY),
        ],
        out_specs=pl.BlockSpec(memory_space=pl.ANY),
        scratch_shapes=[
            pltpu.SMEM((2, 4), F32),
            pltpu.VMEM((6, 64, 128), F32),
            pltpu.VMEM((5, 36, 8, 128), F32),
            pltpu.VMEM((5, 6, 8, 128), F32),
            pltpu.VMEM((5, 8, 128), F32),
            pltpu.VMEM((3, 12, 4, 8, 128), F32),
            pltpu.VMEM((1536, 512), BF16),
            pltpu.VMEM((512, 384), BF16),
            pltpu.VMEM((16, 32, 128), F32),
            pltpu.VMEM((512, 256), BF16),
            pltpu.VMEM((8, 96, 128), F32),
            pltpu.VMEM((8, 96, 128), F32),
            pltpu.VMEM((384, 128), BF16),
            pltpu.VMEM((64, 8, 128), F32),
            pltpu.SemaphoreType.DMA((3,)),
            pltpu.SemaphoreType.DMA((5,)),
        ],
        compiler_params=pltpu.CompilerParams(
            collective_id=0, has_side_effects=True, vmem_limit_bytes=60 * 2**20
        ),
    )(traces, phase_coef, jnp.asarray(tail_table()))


def solution(mesh):
    placed = (P(("gx", "gy"), None), P())
    return jax.shard_map(
        shards, mesh=mesh, in_specs=placed, out_specs=P(("gx", "gy"), None), check_vma=False
    )
```

profile of v0, /device:TPU:9, one launch (start us, length us, event | category | flops | bytes accessed | tf_op | source)
XLA Modules:
  0.0 27.1 jit_solution(14629272818286966987)
XLA Ops:
  0.0 25.5 %shard_map.37 = f32[32,2048]{1,0:T(8,128)} custom-call(f32[32,2048]{1,0:T(8,128)} %x_ref.1, f32[2,4]{1,0:T(2,128)} %coef_hbm.1, f32[6,64,128]{2,1,0:T(8,128)} %constant.2.clone.tail_hbm), custom_call_target="tpu_custom_call" | custom-call | tf_op jit(solution)/shard_map/pallas_call | solution.py:587
  25.5 1.7 %copy.5 = f32[32,2048]{1,0:T(8,128)} copy(f32[32,2048]{1,0:T(8,128)} %shard_map.37) | data formatting | bytes 524288
where the time goes:
time: 27.5 us; the launch traced here: 27.1 us
  Pallas kernels  25.5 us (93%)
  local copies, waits for them, and re-layouts  1.67 us (6%)
    pallas_call x1, Pallas kernels, shards(): pl.pallas_call(kernel, out_shape=jax.ShapeDtypeStruct((32, 2048), F32), i...  25.5 us
    unnamed x1, local copies, waits for them, and re-layouts  1.67 us

commit v1 on v0

--- a/solution.py
+++ b/solution.py
@@ -427,9 +427,6 @@
         pl.semaphore_signal(barrier, inc=1, device_id=source, device_id_type=LOGICAL)
     for mask in range(1, 8):
         pl.semaphore_signal(barrier, inc=1, device_id=me + subset(to_group, mask), device_id_type=LOGICAL)
-    box, top = lane_parts(classes, core)
-    fetch_coef.wait()
-    late_setup(coef_ref, box, top, w_ref, p_ref, c_ref)
     pl.semaphore_wait(barrier, 22)
 
     def columns(m):
@@ -453,6 +450,9 @@
                 device_id_type=LOGICAL,
             ).start()
     pltpu.make_async_copy(columns(block), xr_ref.at[own_slot], recv_sems.at[0]).start()
+    box, top = lane_parts(classes, core)
+    fetch_coef.wait()
+    late_setup(coef_ref, box, top, w_ref, p_ref, c_ref)
     early_levels(coef_ref, box, top, w_ref, p_ref, v_ref)
 
     def order(h):

time: 27.5 us -> 27.7 us (level)
  no operation moved by 1% of the time
where the time goes in v1:
time: 27.7 us; the launch traced here: 27.1 us
  Pallas kernels  25.4 us (92%)
  local copies, waits for them, and re-layouts  1.67 us (6%)
    pallas_call x1, Pallas kernels, shards(): pl.pallas_call(kernel, out_shape=jax.ShapeDtypeStruct((32, 2048), F32), i...  25.4 us
    unnamed x1, local copies, waits for them, and re-layouts  1.67 us

profile of v1, /device:TPU:9, one launch (start us, length us, event | category | flops | bytes accessed | tf_op | source)
XLA Modules:
  0.0 27.1 jit_solution(2561916728191378651)
XLA Ops:
  0.0 25.4 %shard_map.37 = f32[32,2048]{1,0:T(8,128)} custom-call(f32[32,2048]{1,0:T(8,128)} %x_ref.1, f32[2,4]{1,0:T(2,128)} %coef_hbm.1, f32[6,64,128]{2,1,0:T(8,128)} %constant.2.clone.tail_hbm), custom_call_target="tpu_custom_call" | custom-call | tf_op jit(solution)/shard_map/pallas_call | solution.py:587
  25.4 1.7 %copy.5 = f32[32,2048]{1,0:T(8,128)} copy(f32[32,2048]{1,0:T(8,128)} %shard_map.37) | data formatting | bytes 524288

commit v2 on v0

--- a/solution.py
+++ b/solution.py
@@ -544,9 +544,14 @@
     def settle(high):
         return jnp.where(high == early[0], instead[0], jnp.where(high == early[1], instead[1], high))
 
-    tile_ref[...] = jnp.dot(h_ref[...], sum_ref[...], preferred_element_type=F32).reshape(64, 8, 128)
+    def make(start, end):
+        tiles = jnp.dot(h_ref[8 * start : 8 * end, :], sum_ref[...], preferred_element_type=F32)
+        tile_ref[start:end] = tiles.reshape(end - start, 8, 128)
+
+    make(0, 16)
     for high in early:
         pl.when(jnp.logical_or(home != high, jnp.logical_not(own)))(functools.partial(deliver, high))
+    make(16, 64)
     moved = jnp.logical_or(home == early[0], home == early[1])
     last = jnp.logical_or(moved, jnp.logical_not(own))
 

time: 27.5 us -> 27.4 us (level)
  no operation moved by 1% of the time
where the time goes in v2:
time: 27.4 us; the launch traced here: 27.3 us
  Pallas kernels  25.6 us (93%)
  local copies, waits for them, and re-layouts  1.67 us (6%)
    pallas_call x1, Pallas kernels, shards(): pl.pallas_call(kernel, out_shape=jax.ShapeDtypeStruct((32, 2048), F32), i...  25.6 us
    unnamed x1, local copies, waits for them, and re-layouts  1.67 us

profile of v2, /device:TPU:9, one launch (start us, length us, event | category | flops | bytes accessed | tf_op | source)
XLA Modules:
  0.0 27.3 jit_solution(387843911044230407)
XLA Ops:
  0.0 25.6 %shard_map.37 = f32[32,2048]{1,0:T(8,128)} custom-call(f32[32,2048]{1,0:T(8,128)} %x_ref.1, f32[2,4]{1,0:T(2,128)} %coef_hbm.1, f32[6,64,128]{2,1,0:T(8,128)} %constant.2.clone.tail_hbm), custom_call_target="tpu_custom_call" | custom-call | tf_op jit(solution)/shard_map/pallas_call | solution.py:592
  25.6 1.7 %copy.5 = f32[32,2048]{1,0:T(8,128)} copy(f32[32,2048]{1,0:T(8,128)} %shard_map.37) | data formatting | bytes 524288

commit v3 on v2

--- a/solution.py
+++ b/solution.py
@@ -389,8 +389,6 @@
 ):
     fetch_coef = pltpu.make_async_copy(coef_hbm, coef_ref, recv_sems.at[3])
     fetch_tail = pltpu.make_async_copy(tail_hbm, tail_ref, recv_sems.at[4])
-    fetch_coef.start()
-    fetch_tail.start()
     gx, gy = lax.axis_index("gx"), lax.axis_index("gy")
     core = rem(gy, 2)
     zl, xs = div(gx, 4), rem(gx, 4)
@@ -427,9 +425,8 @@
         pl.semaphore_signal(barrier, inc=1, device_id=source, device_id_type=LOGICAL)
     for mask in range(1, 8):
         pl.semaphore_signal(barrier, inc=1, device_id=me + subset(to_group, mask), device_id_type=LOGICAL)
-    box, top = lane_parts(classes, core)
-    fetch_coef.wait()
-    late_setup(coef_ref, box, top, w_ref, p_ref, c_ref)
+    fetch_coef.start()
+    fetch_tail.start()
     pl.semaphore_wait(barrier, 22)
 
     def columns(m):
@@ -453,6 +450,9 @@
                 device_id_type=LOGICAL,
             ).start()
     pltpu.make_async_copy(columns(block), xr_ref.at[own_slot], recv_sems.at[0]).start()
+    box, top = lane_parts(classes, core)
+    fetch_coef.wait()
+    late_setup(coef_ref, box, top, w_ref, p_ref, c_ref)
     early_levels(coef_ref, box, top, w_ref, p_ref, v_ref)
 
     def order(h):

time: 27.4 us -> 27.5 us (level)
  no operation moved by 1% of the time
where the time goes in v3:
time: 27.5 us; the launch traced here: 27.2 us
  Pallas kernels  25.5 us (93%)
  local copies, waits for them, and re-layouts  1.67 us (6%)
    pallas_call x1, Pallas kernels, shards(): pl.pallas_call(kernel, out_shape=jax.ShapeDtypeStruct((32, 2048), F32), i...  25.5 us
    unnamed x1, local copies, waits for them, and re-layouts  1.67 us

profile of v3, /device:TPU:9, one launch (start us, length us, event | category | flops | bytes accessed | tf_op | source)
XLA Modules:
  0.0 27.2 jit_solution(327312931350316393)
XLA Ops:
  0.0 25.5 %shard_map.37 = f32[32,2048]{1,0:T(8,128)} custom-call(f32[32,2048]{1,0:T(8,128)} %x_ref.1, f32[2,4]{1,0:T(2,128)} %coef_hbm.1, f32[6,64,128]{2,1,0:T(8,128)} %constant.2.clone.tail_hbm), custom_call_target="tpu_custom_call" | custom-call | tf_op jit(solution)/shard_map/pallas_call | solution.py:592
  25.5 1.7 %copy.5 = f32[32,2048]{1,0:T(8,128)} copy(f32[32,2048]{1,0:T(8,128)} %shard_map.37) | data formatting | bytes 524288

commit v4 on v2

--- a/solution.py
+++ b/solution.py
@@ -430,6 +430,7 @@
     box, top = lane_parts(classes, core)
     fetch_coef.wait()
     late_setup(coef_ref, box, top, w_ref, p_ref, c_ref)
+    early_levels(coef_ref, box, top, w_ref, p_ref, v_ref)
     pl.semaphore_wait(barrier, 22)
 
     def columns(m):
@@ -453,7 +454,6 @@
                 device_id_type=LOGICAL,
             ).start()
     pltpu.make_async_copy(columns(block), xr_ref.at[own_slot], recv_sems.at[0]).start()
-    early_levels(coef_ref, box, top, w_ref, p_ref, v_ref)
 
     def order(h):
         return classes[0] + (1 - h) * (1 - 2 * classes[0])

time: 27.4 us -> 27.4 us (level)
  no operation moved by 1% of the time
where the time goes in v4:
time: 27.4 us; the launch traced here: 27.2 us
  Pallas kernels  25.5 us (93%)
  local copies, waits for them, and re-layouts  1.67 us (6%)
    pallas_call x1, Pallas kernels, shards(): pl.pallas_call(kernel, out_shape=jax.ShapeDtypeStruct((32, 2048), F32), i...  25.5 us
    unnamed x1, local copies, waits for them, and re-layouts  1.67 us

profile of v4, /device:TPU:9, one launch (start us, length us, event | category | flops | bytes accessed | tf_op | source)
XLA Modules:
  0.0 27.2 jit_solution(3557413691599994080)
XLA Ops:
  0.0 25.5 %shard_map.37 = f32[32,2048]{1,0:T(8,128)} custom-call(f32[32,2048]{1,0:T(8,128)} %x_ref.1, f32[2,4]{1,0:T(2,128)} %coef_hbm.1, f32[6,64,128]{2,1,0:T(8,128)} %constant.2.clone.tail_hbm), custom_call_target="tpu_custom_call" | custom-call | tf_op jit(solution)/shard_map/pallas_call | solution.py:592
  25.6 1.7 %copy.5 = f32[32,2048]{1,0:T(8,128)} copy(f32[32,2048]{1,0:T(8,128)} %shard_map.37) | data formatting | bytes 524288
